TPU v7x, 256 devices: a whole 4x4x8 slice. The times are simulated.
256 devices in a mesh: seq: 64 (over z, x, core), mp: 4 (over y).
Axes of the slice: x: 4, y: 4, z: 8, core: 2. Of those that a mesh axis runs over, the one named last changes fastest.
Arguments:
- tokens: bfloat16 [32768, 5120], P('seq'), may hold values from -6 to 6
- ln1_gain: float32 [5120], replicated, may hold values from 0.25 to 1.75
- w_query: bfloat16 [5120, 2560], P('seq', 'mp'), may hold values from -1 to 1
- w_key: bfloat16 [5120, 2560], P('seq', 'mp'), may hold values from -1 to 1
- w_value: bfloat16 [5120, 2560], P('seq', 'mp'), may hold values from -0.078125 to 0.078125
- w_out: bfloat16 [2560, 5120], P(None, 'mp'), may hold values from -0.125 to 0.125
- segment_ids: int32 [64, 512], P('seq'), may hold values from 0 to 7, never falling along the last dimension, each value on 1 to 256 neighbouring positions
- lnf_gain: float32 [5120], P('mp'), may hold values from 0.25 to 1.75
- w_pair: bfloat16 [5120, 64], P('mp'), may hold values from -0.078125 to 0.078125
- pair_start: int32 [1], replicated, may hold values from 0 to 32256
- residue_mask: int32 [512], replicated, may hold values 0 or 1
- w_pair_out: bfloat16 [64, 128], replicated, may hold values from -0.75 to 0.75
- rel_table: float32 [65, 128], replicated, may hold values from -6 to 6
- tri_gain: float32 [128], replicated, may hold values from 0.25 to 1.75
- w_ap: bfloat16 [128, 64], P(None, 'mp'), may hold values from -0.5 to 0.5
- w_ag: bfloat16 [128, 64], P(None, 'mp'), may hold values from -0.5 to 0.5
- w_bp: bfloat16 [128, 64], P(None, 'mp'), may hold values from -0.5 to 0.5
- w_bg: bfloat16 [128, 64], P(None, 'mp'), may hold values from -0.5 to 0.5
- w_gate: bfloat16 [128, 128], replicated, may hold values from -0.5 to 0.5
- out_gain: float32 [64], replicated, may hold values from 0.25 to 1.75
- w_tri_out: bfloat16 [64, 128], replicated, may hold values from -0.75 to 0.75
Outputs:
- final_states: bfloat16 [32768, 5120], P('seq', 'mp')
- pair_update: bfloat16 [512, 512, 128], P('seq', 'mp')
Inputs may be any that keep to these rules, and one draw needn't show every extreme that they name: `segment_ids`: within each packed row the ids never fall; each protein has at most 256 tokens.
All inputs are finite; a program needn't handle non-finite values.
Results may differ from a plain program's by a relative error of at most 0.011.
Values may be sent and summed in bfloat16 or wider, within the bound.
No kernel may reach another device: no remote copies, remote signals or barrier semaphores. Data moves between devices by JAX's collectives and lax.ppermute only.
A program may use at most 128 MiB of HBM per device.

v0:
```python
import jax
import jax.numpy as jnp
from jax import lax
from jax.sharding import PartitionSpec as P

HD = 128


EPS = 1e-05


def norm_rows(values, gain):
    center = values - jnp.mean(values, axis=-1, keepdims=True)
    spread = jnp.mean(center * center, axis=-1, keepdims=True)
    return center * lax.rsqrt(spread + EPS) * gain


def rotate(tensor, positions):
    half = tensor.shape[-1] // 2
    freqs = 10000.0 ** (-2.0 * jnp.arange(half, dtype=jnp.float32) / tensor.shape[-1])
    angles = positions.astype(jnp.float32)[:, None] * freqs[None, :]
    cosine = jnp.concatenate([jnp.cos(angles), jnp.cos(angles)], axis=-1)[:, None, :]
    sine = jnp.concatenate([jnp.sin(angles), jnp.sin(angles)], axis=-1)[:, None, :]
    turned = jnp.concatenate([-tensor[..., half:], tensor[..., :half]], axis=-1)
    return tensor * cosine + turned * sine


def attend(query_all, key_all, value_all, seg_row, head_dim):
    count = query_all.shape[0]
    heads = query_all.shape[1] // head_dim
    smaller = (seg_row[None, :] < seg_row[:, None]).astype(jnp.int32)
    positions = jnp.arange(count, dtype=jnp.int32) - jnp.sum(smaller, axis=1)
    queries = rotate(query_all.reshape(count, heads, head_dim), positions).astype(jnp.bfloat16)
    key_rows = rotate(key_all.reshape(count, heads, head_dim), positions).astype(jnp.bfloat16)
    value_rows = value_all.reshape(count, heads, head_dim).astype(jnp.bfloat16)
    scores = jnp.einsum(
        "qhd,khd->hqk", queries, key_rows, preferred_element_type=jnp.float32
    ) * head_dim ** (-0.5)
    same = seg_row[:, None] == seg_row[None, :]
    scores = jnp.where(same[None, :, :], scores, -1e30)
    top = jnp.max(scores, axis=-1, keepdims=True)
    expo = jnp.exp(scores - top)
    weights = (expo / jnp.sum(expo, axis=-1, keepdims=True)).astype(jnp.bfloat16)
    mixed = jnp.einsum("hqk,khd->qhd", weights, value_rows, preferred_element_type=jnp.float32)
    return mixed.astype(jnp.bfloat16).reshape(count, heads * head_dim)


def pair_block(pair_in, start, count, w_pair_out, rel_table, tri_gain):
    width = pair_in.shape[1] // 2
    left = lax.dynamic_slice_in_dim(pair_in[:, :width], start, count, 0)
    right = pair_in[:, width:]
    total = right.shape[0]
    features = jnp.concatenate(
        [left[:, None, :] * right[None, :, :], left[:, None, :] - right[None, :, :]], axis=-1
    )
    grid = jnp.einsum(
        "ijf,fc->ijc", features, w_pair_out.astype(jnp.float32), precision=lax.Precision.HIGHEST
    )
    reach = (rel_table.shape[0] - 1) // 2
    offsets = (
        jnp.arange(total, dtype=jnp.int32)[None, :]
        - (start + jnp.arange(count, dtype=jnp.int32))[:, None]
    )
    bins = jnp.clip(offsets, -reach, reach) + reach
    onehot = (bins[..., None] == jnp.arange(rel_table.shape[0], dtype=jnp.int32)).astype(
        jnp.float32
    )
    grid = grid + jnp.einsum("ijr,rc->ijc", onehot, rel_table, precision=lax.Precision.HIGHEST)
    pair_grid = grid.astype(jnp.bfloat16)
    normed = norm_rows(pair_grid.astype(jnp.float32), tri_gain).astype(jnp.bfloat16)
    return (pair_grid, normed)


def gated(normed, w_proj, w_gate_in, row_mask, col_mask):
    gate = jax.nn.sigmoid(jnp.dot(normed, w_gate_in, preferred_element_type=jnp.float32))
    projected = jnp.dot(normed, w_proj, preferred_element_type=jnp.float32)
    both = (row_mask[:, None] * col_mask[None, :])[..., None]
    return (gate * projected * both).astype(jnp.bfloat16)


def shards(
    tokens,
    ln1_gain,
    w_query,
    w_key,
    w_value,
    w_out,
    segment_ids,
    lnf_gain,
    w_pair,
    pair_start,
    residue_mask,
    w_pair_out,
    rel_table,
    tri_gain,
    w_ap,
    w_ag,
    w_bp,
    w_bg,
    w_gate,
    out_gain,
    w_tri_out,
):
    seq_index = lax.axis_index("seq")
    mp_index = lax.axis_index("mp")
    count = tokens.shape[0]
    normed_tokens = norm_rows(tokens.astype(jnp.float32), ln1_gain).astype(jnp.bfloat16)
    pieces = (
        lax.all_gather(w_query, "seq", axis=0, tiled=True),
        lax.all_gather(w_key, "seq", axis=0, tiled=True),
        lax.all_gather(w_value, "seq", axis=0, tiled=True),
    )
    query_all, key_all, value_all = tuple(
        (jnp.dot(normed_tokens, piece, preferred_element_type=jnp.float32) for piece in pieces)
    )
    mixed = attend(query_all, key_all, value_all, segment_ids[0], HD)
    all_heads = lax.all_gather(mixed, "mp", axis=1, tiled=True)
    local_width = w_out.shape[1]
    residual = lax.dynamic_slice_in_dim(tokens, mp_index * local_width, local_width, 1)
    final_states = (
        residual.astype(jnp.float32) + jnp.dot(all_heads, w_out, preferred_element_type=jnp.float32)
    ).astype(jnp.bfloat16)
    residues = residue_mask.shape[0]
    wanted = pair_start[0] + jnp.arange(residues, dtype=jnp.int32)
    held = seq_index * count + jnp.arange(count, dtype=jnp.int32)
    picker = (wanted[:, None] == held[None, :]).astype(jnp.bfloat16)
    chosen = jnp.dot(picker, final_states, preferred_element_type=jnp.float32)
    pair_weight = w_pair.astype(jnp.float32)
    partial_value = jnp.dot(chosen * lnf_gain, pair_weight, precision=lax.Precision.HIGHEST)
    first = jnp.sum(chosen, axis=1)
    second = jnp.sum(chosen * chosen, axis=1)
    shift_row = jnp.dot(lnf_gain, pair_weight, precision=lax.Precision.HIGHEST) * (
        seq_index == 0
    ).astype(jnp.float32)
    partial_value, first, second, shift_row = lax.psum(
        (partial_value, first, second, shift_row), ("seq", "mp")
    )
    full_width = lnf_gain.shape[0] * lax.axis_size("mp")
    center = first / full_width
    spread = second / full_width - center * center
    pair_in = (partial_value - center[:, None] * shift_row[None, :]) * lax.rsqrt(spread + EPS)[
        :, None
    ]
    rows = residues // lax.axis_size("seq")
    row_start = seq_index * rows
    pair_grid, normed = pair_block(pair_in, row_start, rows, w_pair_out, rel_table, tri_gain)
    mask = residue_mask.astype(jnp.float32)
    row_mask = lax.dynamic_slice_in_dim(mask, row_start, rows, 0)
    left_side = gated(normed, w_ap, w_ag, row_mask, mask)
    right_own = gated(normed, w_bp, w_bg, row_mask, mask)
    product = jnp.einsum(
        "ikc,jkc->ijc",
        left_side,
        lax.all_gather(right_own, "seq", axis=0, tiled=True),
        preferred_element_type=jnp.float32,
    )
    col_span = residues // lax.axis_size("mp")
    col_start = mp_index * col_span
    own_grid = lax.dynamic_slice_in_dim(pair_grid, col_start, col_span, 1)
    own_normed = lax.dynamic_slice_in_dim(normed, col_start, col_span, 1)
    gate_out = jax.nn.sigmoid(jnp.dot(own_normed, w_gate, preferred_element_type=jnp.float32))
    out_weight = w_tri_out.astype(jnp.float32)
    local_channels = product.shape[2]
    channel_start = mp_index * local_channels
    gain_own = lax.dynamic_slice_in_dim(out_gain, channel_start, local_channels, 0)
    weight_own = lax.dynamic_slice_in_dim(out_weight, channel_start, local_channels, 0)
    partial_out = jnp.einsum(
        "ijc,cd->ijd", product * gain_own, weight_own, precision=lax.Precision.HIGHEST
    )
    first_out = jnp.sum(product, axis=-1)
    second_out = jnp.sum(product * product, axis=-1)
    partial_out, first_out, second_out = (
        lax.psum_scatter(
            partial_out.astype(jnp.bfloat16), "mp", scatter_dimension=1, tiled=True
        ).astype(jnp.float32),
        lax.psum_scatter(
            first_out.astype(jnp.bfloat16), "mp", scatter_dimension=1, tiled=True
        ).astype(jnp.float32),
        lax.psum_scatter(
            second_out.astype(jnp.bfloat16), "mp", scatter_dimension=1, tiled=True
        ).astype(jnp.float32),
    )
    shift_out = jnp.dot(out_gain, out_weight, precision=lax.Precision.HIGHEST)
    hidden_width = out_gain.shape[0]
    mean_out = first_out / hidden_width
    var_out = second_out / hidden_width - mean_out * mean_out
    update = (partial_out - mean_out[..., None] * shift_out) * lax.rsqrt(var_out + EPS)[..., None]
    pair_update = (own_grid.astype(jnp.float32) + gate_out * update).astype(jnp.bfloat16)
    return (final_states, pair_update)


def solution(mesh):
    return jax.shard_map(
        shards,
        mesh=mesh,
        in_specs=(
            P("seq", None),
            P(),
            P("seq", "mp"),
            P("seq", "mp"),
            P("seq", "mp"),
            P(None, "mp"),
            P("seq", None),
            P("mp"),
            P("mp", None),
            P(),
            P(),
            P(),
            P(),
            P(),
            P(None, "mp"),
            P(None, "mp"),
            P(None, "mp"),
            P(None, "mp"),
            P(),
            P(),
            P(),
        ),
        out_specs=(P("seq", "mp"), P("seq", "mp", None)),
        check_vma=False,
    )
```

profile of v0, /device:TPU:2, one launch (start us, length us, event | category | flops | bytes accessed | tf_op | source)
XLA Modules:
  0.0 739.0 jit_solution(1601630111425255341)
XLA Ops:
  9.5 0.9 convert_reduce_fusion.2
  11.0 3.4 convert_reduce_fusion
  15.1 1.5 fusion.3
  16.6 0.9 broadcast_compare_fusion
  17.5 5.3 fusion.5
  22.8 71.1 %all-gather.6.cloned.1.call-done = bf16[5120,640]{1,0:T(8,128)(2,1)} async-done(((bf16[80,640]{1,0:T(8,128)(2,1)}), bf16[5120,640]{1,0:T(8,128)(2,1)}) %all-gather.6.cloned.1.call-update) | async-done | bytes 6553616 | tf_op jit(solution)/shard_map/all_gather | solution.py:111
  93.8 8.6 %convolution_convert_fusion.1 = bf16[512,640]{1,0:T(8,128)(2,1)S(1)} fusion(bf16[512,5120]{1,0:T(8,128)(2,1)} %fusion.5, bf16[5120,640]{1,0:T(8,128)(2,1)} %all-gather.6.cloned.1.call-done), kind=kOutput, calls=%fused_computation.33 | convolution fusion | flops 3355770880 | bytes 12451840 | tf_op jit(solution)/shard_map/dot_general | solution.py:114
  102.5 1.1 copy.67
  103.6 71.0 %all-gather.10.cloned.1.call-done = bf16[5120,640]{1,0:T(8,128)(2,1)} async-done(((bf16[80,640]{1,0:T(8,128)(2,1)}), bf16[5120,640]{1,0:T(8,128)(2,1)}) %all-gather.10.cloned.1.call-update) | async-done | bytes 6553616 | tf_op jit(solution)/shard_map/all_gather | solution.py:110
  174.5 8.6 %fusion.85 = f32[512,640]{0,1:T(8,128)S(1)} fusion(bf16[512,5120]{1,0:T(8,128)(2,1)} %fusion.5, bf16[5120,640]{1,0:T(8,128)(2,1)} %all-gather.10.cloned.1.call-done), kind=kOutput, calls=%fused_computation.133 | convolution fusion | flops 3355443200 | bytes 13107200 | tf_op jit(solution)/shard_map/dot_general | solution.py:114
  183.3 72.0 %all-gather.8.cloned.1.call-done = bf16[5120,640]{1,0:T(8,128)(2,1)} async-done(((bf16[80,640]{1,0:T(8,128)(2,1)}), bf16[5120,640]{1,0:T(8,128)(2,1)}) %all-gather.8.cloned.1.call-update) | async-done | bytes 6553616 | tf_op jit(solution)/shard_map/all_gather | solution.py:109
  255.3 8.4 %fusion.84 = f32[512,640]{0,1:T(8,128)S(1)} fusion(bf16[512,5120]{1,0:T(8,128)(2,1)} %fusion.5, bf16[5120,640]{1,0:T(8,128)(2,1)} %all-gather.8.cloned.1.call-done), kind=kOutput, calls=%fused_computation.132 | convolution fusion | flops 3355443200 | bytes 13107200 | tf_op jit(solution)/shard_map/dot_general | solution.py:114
  263.8 1.1 fusion.53
  264.9 2.5 fusion.83
  267.5 1.4 fusion.21
  270.3 1.3 fusion.33
  271.5 33.1 %all-gather.12.cloned.1.call-done = bf16[512,2560]{0,1:T(8,128)(2,1)} async-done(((bf16[512,640]{0,1:T(8,128)(2,1)}), bf16[512,2560]{0,1:T(8,128)(2,1)}) %all-gather.12.cloned.1.call-update) | async-done | bytes 2621456 | tf_op jit(solution)/shard_map/all_gather | solution.py:117
  304.6 7.7 %fusion.9 = bf16[512,1280]{1,0:T(8,128)(2,1)S(1)} fusion(bf16[512,2560]{0,1:T(8,128)(2,1)} %all-gather.12.cloned.1.call-done, bf16[2560,1280]{1,0:T(8,128)(2,1)} %param.26, bf16[512,5120]{1,0:T(8,128)(2,1)} %param.21, s32[]{:T(128)S(6)} %select_n.19), kind=kOutput, calls=%fused_computation.15 | convolution fusion | flops 3357409280 | bytes 11796484 | tf_op jit(solution)/shard_map/dot_general | solution.py:121
  312.3 1.0 fusion.80
  313.4 2.2 fusion.10
  315.7 75.6 %all-reduce = (f32[512]{0:T(512)S(1)}, f32[512]{0:T(512)S(1)}, f32[64]{0:T(128)S(1)}) all-reduce(f32[512]{0:T(512)S(1)} %get-tuple-element.11, f32[512]{0:T(512)S(1)} %get-tuple-element.10, f32[64]{0:T(128)S(1)} %fusion.47), channel_id=1, replica_groups=mesh['seq'=64,'mp'=4] {'seq','mp'}, use_global_device_ids=true, to_apply=%region_10.11 | all-reduce | flops 1088 | bytes 8704 | tf_op jit(solution)/shard_map/psum | solution.py:135
  391.3 166.5 %all-reduce.3.cloned.1.call-done = f32[512,64]{0,1:T(8,128)} async-done(((f32[512,64]{0,1:T(8,128)}), f32[512,64]{0,1:T(8,128)}) %all-reduce.3.cloned.1.call-update) | async-done | bytes 131088 | tf_op jit(solution)/shard_map/psum | solution.py:135
  557.8 1.0 subtract_multiply_fusion
  559.1 1.3 convert_reduce_fusion.1
  563.3 77.5 %all-gather.14.cloned.1.call-done = bf16[512,512,16]{1,2,0:T(8,128)(2,1)} async-done(((bf16[8,512,16]{1,2,0:T(8,128)(2,1)}), bf16[512,512,16]{1,2,0:T(8,128)(2,1)}) %all-gather.14.cloned.1.call-update) | async-done | bytes 8388624 | tf_op jit(solution)/shard_map/all_gather | solution.py:154
  640.8 12.2 %fusion.81 = (bf16[8,512]{1,0:T(8,128)(2,1)S(1)}, bf16[8,512]{1,0:T(8,128)(2,1)S(1)}, f32[8,512,16]{1,0,2:T(8,128)S(1)}) fusion(f32[16]{0:T(128)S(1)} %dynamic_slice.26, bf16[8,512,16]{1,2,0:T(8,128)(2,1)S(1)} %fusion.45, bf16[512,512,16]{1,2,0:T(8,128)(2,1)} %all-gather.14.cloned.1.call-done), kind=kOutput, calls=%fused_computation.129 | convolution fusion | flops 67362816 | bytes 8798272 | tf_op jit(solution)/shard_map/ikc,jkc->ijc/dot_general | solution.py:151
  655.2 1.8 convolution_convert_fusion
  657.7 1.3 copy.118
  659.1 16.5 %reduce-scatter.12.cloned.1.call-done = bf16[128,8]{1,0:T(8,128)(2,1)} async-done(((bf16[512,8]{1,0:T(8,128)(2,1)}), bf16[128,8]{1,0:T(8,128)(2,1)}) %reduce-scatter.12.cloned.1.call-update) | async-done | bytes 2064
  676.4 24.6 %reduce-scatter.14.cloned.1.call-done = bf16[128,8]{1,0:T(8,128)(2,1)} async-done(((bf16[512,8]{1,0:T(8,128)(2,1)}), bf16[128,8]{1,0:T(8,128)(2,1)}) %reduce-scatter.14.cloned.1.call-update) | async-done | bytes 2064
  701.8 27.6 %reduce-scatter.10.cloned.1.call-done = bf16[128,1024]{1,0:T(8,128)(2,1)} async-done(((bf16[512,1024]{1,0:T(8,128)(2,1)}), bf16[128,1024]{1,0:T(8,128)(2,1)}) %reduce-scatter.10.cloned.1.call-update) | async-done | bytes 262160
  729.5 1.0 copy.104
  (96 shorter events, 13.6 us)
Async XLA Ops:
  7.2 262.9 %copy-start = (bf16[1280,64]{0,1:T(8,128)(2,1)S(1)}, bf16[1280,64]{0,1:T(8,128)(2,1)}, u32[]{:S(2)}) copy-start(bf16[1280,64]{0,1:T(8,128)(2,1)} %param.29) | copy-start | bytes 491524
  7.2 86.7 %all-gather.6.cloned.1.call-start = ((), (), s32[]{:S(2)}) async-start(), calls=%async_computation.3 | async-start | bytes 6656000 | tf_op jit(solution)/shard_map/all_gather | solution.py:111
  7.9 166.6 %all-gather.10.cloned.1.call-start = ((), (), s32[]{:S(2)}) async-start(), calls=%async_computation.5 | async-start | bytes 6656000 | tf_op jit(solution)/shard_map/all_gather | solution.py:110
  8.7 246.6 %all-gather.8.cloned.1.call-start = ((), (), s32[]{:S(2)}) async-start(), calls=%async_computation.4 | async-start | bytes 6656000 | tf_op jit(solution)/shard_map/all_gather | solution.py:109
  9.4 295.2 %all-gather.12.cloned.1.call-start = ((), (), s32[]{:S(2)}) async-start(), calls=%async_computation.6 | async-start | bytes 3276800 | tf_op jit(solution)/shard_map/all_gather | solution.py:117
  11.0 4.0 copy-start.1
  15.1 1.5 copy-start.6
  15.1 2.4 copy-start.7
  263.8 1.1 copy-start.3
  264.9 2.6 copy-start.2
  267.4 2.3 copy-start.5
  267.5 2.4 copy-start.11
  267.5 2.8 copy-start.4
  268.9 288.9 %all-reduce.3.cloned.1.call-start = ((), (), s32[]{:S(2)}) async-start(), calls=%async_computation.7 | async-start | bytes 262144 | tf_op jit(solution)/shard_map/psum | solution.py:135
  312.3 1.1 copy-start.18
  313.4 245.7 %copy-start.8 = (bf16[64,128]{1,0:T(8,128)(2,1)S(1)}, bf16[64,128]{1,0:T(8,128)(2,1)}, u32[]{:S(2)}) copy-start(bf16[64,128]{1,0:T(8,128)(2,1)} %param.32) | copy-start | bytes 49156
  315.6 325.2 %all-gather.14.cloned.1.call-start = ((), (), s32[]{:S(2)}) async-start(), calls=%async_computation.8 | async-start | bytes 8519680 | tf_op jit(solution)/shard_map/all_gather | solution.py:154
  559.1 1.6 copy-start.13
  560.4 0.8 copy-start.15
  560.4 1.1 copy-start.9
  560.7 2.0 copy-start.17
  560.8 2.0 copy-start.16
  561.2 1.9 copy-start.10
  562.4 113.2 %reduce-scatter.12.cloned.1.call-start = ((), (), s32[]{:S(2)}) async-start(), calls=%async_computation.10 | async-start | bytes 163840
  563.3 91.8 %copy-start.12 = (bf16[64,128]{1,0:T(8,128)(2,1)S(1)}, bf16[64,128]{1,0:T(8,128)(2,1)}, u32[]{:S(2)}) copy-start(bf16[64,128]{1,0:T(8,128)(2,1)} %param.41) | copy-start | bytes 49156
  654.0 47.1 %reduce-scatter.14.cloned.1.call-start = ((), (), s32[]{:S(2)}) async-start(), calls=%async_computation.11 | async-start | bytes 163840
  654.8 74.7 %reduce-scatter.10.cloned.1.call-start = ((), (), s32[]{:S(2)}) async-start(), calls=%async_computation.9 | async-start | bytes 1310720
  657.7 73.0 %copy-start.14 = (bf16[128,128]{1,0:T(8,128)(2,1)S(1)}, bf16[128,128]{1,0:T(8,128)(2,1)}, u32[]{:S(2)}) copy-start(bf16[128,128]{1,0:T(8,128)(2,1)} %param.39) | copy-start | bytes 98308
Sparse Core Ops, SparseCore 0:
  10.7 83.0 all-gather.5
  96.5 77.9 all-gather.9
  177.2 77.9 all-gather.7
  269.0 35.5 all-gather.11
  315.7 241.9 all-reduce.2
  562.5 78.2 all-gather.13
  654.1 21.4 reduce-scatter.11
  678.2 22.7 reduce-scatter.13
  703.6 25.8 reduce-scatter.9
where the time goes:
time: 746 us; the launch traced here: 739 us
  waiting for transfers between devices  562 us (75%)
  blocking collectives  75.6 us (10%)
  matrix products  57.9 us (8%)
  other arithmetic  17.4 us (2%)
  between operations  15.5 us (2%)
  local copies, waits for them, and re-layouts  9.43 us (1%)
    psum x1, waiting for transfers between devices, shards(): lax.psum((partial_value, first, second, shift_row), ('seq', 'mp'))  167 us
    all_gather x1, waiting for transfers between devices, shards(): lax.all_gather(right_own, 'seq', axis=0, tiled=True)  77.5 us
    psum x1, blocking collectives, shards(): lax.psum((partial_value, first, second, shift_row), ('seq', 'mp'))  75.6 us
    all_gather x1, waiting for transfers between devices, shards(): lax.all_gather(w_query, 'seq', axis=0, tiled=True)  72 us
    all_gather x1, waiting for transfers between devices, shards(): lax.all_gather(w_value, 'seq', axis=0, tiled=True)  71.1 us
    all_gather x1, waiting for transfers between devices, shards(): lax.all_gather(w_key, 'seq', axis=0, tiled=True)  71 us
    unnamed x12, waiting for transfers between devices  70.9 us
    all_gather x1, waiting for transfers between devices, shards(): all_heads = lax.all_gather(mixed, 'mp', axis=1, tiled=True)  33.1 us
  transfers between devices with their start and end apart: 9, of which 9 were waited for; matrix products, arithmetic and copies ran while one was open for 5% of the time, Pallas kernels for 0%

commit v1 on v0

v1 whole, which is shorter than its diff:
```python
import functools

import jax
import jax.numpy as jnp
from jax import lax
from jax.experimental import pallas as pl
from jax.experimental.pallas import tpu as pltpu
from jax.sharding import Mesh, PartitionSpec as P

HD = 128
EPS = 1e-05
NZ, NX, NC, NY = 8, 4, 2, 4
SEQ = ("z", "x", "core")
F32, BF16 = jnp.float32, jnp.bfloat16


def shift(value, axis, size, by):
    return lax.ppermute(value, axis, [(i, (i + by) % size) for i in range(size)])


def partner(value, axis, size, bit):
    return lax.ppermute(value, axis, [(i, i ^ bit) for i in range(size)])


def split(value):
    high = lax.reduce_precision(value, 8, 7)
    return high.astype(BF16), (value - high).astype(BF16)


def norm_rows(values, gain):
    center = values - jnp.mean(values, axis=-1, keepdims=True)
    spread = jnp.mean(center * center, axis=-1, keepdims=True)
    return center * lax.rsqrt(spread + EPS) * gain


def rotate(tensor, positions):
    half = tensor.shape[-1] // 2
    freqs = 10000.0 ** (-2.0 * jnp.arange(half, dtype=F32) / tensor.shape[-1])
    angles = positions.astype(F32)[:, None] * freqs[None, :]
    cosine = jnp.concatenate([jnp.cos(angles), jnp.cos(angles)], axis=-1)[:, None, :]
    sine = jnp.concatenate([jnp.sin(angles), jnp.sin(angles)], axis=-1)[:, None, :]
    turned = jnp.concatenate([-tensor[..., half:], tensor[..., :half]], axis=-1)
    return tensor * cosine + turned * sine


def attend(query_all, key_all, value_all, seg_row, head_dim):
    count = query_all.shape[0]
    heads = query_all.shape[1] // head_dim
    smaller = (seg_row[None, :] < seg_row[:, None]).astype(jnp.int32)
    positions = jnp.arange(count, dtype=jnp.int32) - jnp.sum(smaller, axis=1)
    queries = rotate(query_all.reshape(count, heads, head_dim), positions).astype(BF16)
    key_rows = rotate(key_all.reshape(count, heads, head_dim), positions).astype(BF16)
    value_rows = value_all.reshape(count, heads, head_dim).astype(BF16)
    scores = jnp.einsum(
        "qhd,khd->hqk", queries, key_rows, preferred_element_type=F32
    ) * head_dim ** (-0.5)
    same = seg_row[:, None] == seg_row[None, :]
    scores = jnp.where(same[None, :, :], scores, -1e30)
    top = jnp.max(scores, axis=-1, keepdims=True)
    expo = jnp.exp(scores - top)
    weights = (expo / jnp.sum(expo, axis=-1, keepdims=True)).astype(BF16)
    mixed = jnp.einsum("hqk,khd->qhd", weights, value_rows, preferred_element_type=F32)
    return mixed.astype(BF16).reshape(count, heads * head_dim)


def pair_kernel(
    starts, left_ref, rrhs_ref, wp_ref, base_ref, wd_ref, rel_ref, gain_ref,
    wl_ref, wr_ref, wgate_ref, wout_ref, ogain_ref, mask_ref, mask_smem,
    out_ref, side_ref, own_x, own_n,
):
    n_i, n_j, _ = out_ref.shape
    res = rrhs_ref.shape[1]
    ch = side_ref.shape[1]
    i0, j0, tile, half = starts[0], starts[1], starts[2], starts[3]
    lane = lax.broadcasted_iota(jnp.int32, (128, 128), 1)
    const_lane = ((lane == 96) | (lane == 97)).astype(F32)
    low_lane = ((lane >= 64) & (lane < 96)) | (lane == 97)
    bins = lax.broadcasted_iota(jnp.int32, (64, res), 0)
    cols = lax.broadcasted_iota(jnp.int32, (64, res), 1)
    never = 4 * res
    diag = jnp.where(bins == 0, never, cols - bins)
    first_bin = jnp.where(bins == 0, cols, never)

    def grid_row(row):
        left = left_ref[pl.ds(row, 1), :]
        const = jnp.sum(left * wd_ref[...], axis=1, keepdims=True)
        full = left * wp_ref[...] + base_ref[...] + const * const_lane
        high = full.astype(BF16)
        low = (full - high.astype(F32)).astype(BF16)
        coef = jnp.where(low_lane, low.astype(F32), high.astype(F32)).astype(BF16)
        hot = (diag == row - 32) | (first_bin <= row - 32)
        hot = jnp.where(hot, 1.0, 0.0).astype(BF16)
        grid = jnp.dot(
            jnp.concatenate([coef, rel_ref[...]], axis=1),
            jnp.concatenate([rrhs_ref[...], hot, hot], axis=0),
            preferred_element_type=F32,
        )
        x = grid.astype(BF16)
        xf = x.astype(F32)
        center = xf - jnp.mean(xf, axis=0, keepdims=True)
        spread = jnp.mean(center * center, axis=0, keepdims=True)
        normed = (center * lax.rsqrt(spread + EPS) * gain_ref[...]).astype(BF16)
        return x, normed

    def side(normed, weight, row):
        both = jnp.dot(weight, normed, preferred_element_type=F32)
        gate = 0.5 + 0.5 * jnp.tanh(0.5 * both[:ch])
        keep = mask_ref[...] * mask_smem[row].astype(F32)
        return (gate * both[ch:] * keep).astype(BF16)

    def left_row(i, carry):
        x, normed = grid_row(i0 + i)
        side_ref[pl.ds(i, 1)] = side(normed, wl_ref[...], i0 + i)[None]
        own_x[pl.ds(i, 1)] = x[None]
        own_n[pl.ds(i, 1)] = normed[None]
        return carry

    def right_row(j, carry):
        normed = grid_row(j0 + j)[1]
        side_ref[pl.ds(n_i + j, 1)] = side(normed, wr_ref[...], j0 + j)[None]
        return carry

    lax.fori_loop(0, n_i, left_row, 0)
    lax.fori_loop(0, n_j, right_row, 0)

    left_side = jnp.swapaxes(side_ref[:n_i], 0, 1)
    right_side = jnp.swapaxes(side_ref[n_i:], 0, 1)
    product = lax.dot_general(
        left_side, right_side, (((2,), (2,)), ((0,), (0,))), preferred_element_type=F32
    )
    center = product - jnp.mean(product, axis=0, keepdims=True)
    spread = jnp.mean(center * center, axis=0, keepdims=True)
    hidden = center * lax.rsqrt(spread + EPS) * ogain_ref[...]
    hidden = jnp.swapaxes(hidden, 0, 1)
    window = pl.ds(pl.multiple_of(tile * 128, 128), 128)
    contract = (((0,), (0,)), ((), ()))

    def pick(value):
        return jnp.where(half == 0, value[:n_j], value[n_j:])

    for i in range(n_i):
        high = hidden[i].astype(BF16)
        low = (hidden[i] - high.astype(F32)).astype(BF16)
        update = lax.dot_general(
            jnp.concatenate([high, low], axis=0), wout_ref[...], contract,
            preferred_element_type=F32,
        )
        gate = lax.dot_general(
            own_n[i, :, window], wgate_ref[...], contract, preferred_element_type=F32
        )
        gate = 0.5 + 0.5 * jnp.tanh(0.5 * pick(gate))
        grid = pick(own_x[i, :, window].astype(F32).T)
        out_ref[i] = (grid + gate * update).astype(BF16)


def pair_phase(pair_t, w_pair_out, rel_table, tri_gain, sides, w_gate, w_tri_out, out_gain, mask):
    res = pair_t.shape[1]
    width = pair_t.shape[0] // 2
    core = lax.axis_index("core")
    plane = lax.axis_index("z") * NX + lax.axis_index("x")
    n_i, n_j = 16, 64
    starts = jnp.stack(
        [plane * n_i, lax.axis_index("mp") * 128 + core * n_j, lax.axis_index("mp"), core]
    ).astype(jnp.int32)
    left = pair_t[:width].T
    left3 = jnp.concatenate([left, left, left, jnp.zeros((res, 32), F32)], axis=1)
    right_high, right_low = split(pair_t[width:])
    rrhs = jnp.concatenate(
        [right_high, right_low, right_high, jnp.ones((2, res), BF16), jnp.zeros((30, res), BF16)],
        axis=0,
    )
    wp = w_pair_out[:width].astype(F32).T
    wd = w_pair_out[width:].astype(F32).T
    zero = jnp.zeros((128, 32), F32)
    wp3 = jnp.concatenate([wp, wp, wp, zero], axis=1)
    wd1 = jnp.concatenate([wd, zero, zero, zero], axis=1)
    last = rel_table[-1][:, None]
    base = jnp.concatenate([-wd, -wd, -wd, last, last, zero[:, :30]], axis=1)
    rel_high, rel_low = split((rel_table[:-1] - rel_table[-1:]).T)
    rel = jnp.concatenate([rel_high, rel_low], axis=1)
    smem = pl.BlockSpec(memory_space=pltpu.SMEM)
    vmem = pl.BlockSpec(memory_space=pltpu.VMEM)
    block = pl.pallas_call(
        pair_kernel,
        out_shape=jax.ShapeDtypeStruct((n_i, n_j, 128), BF16),
        in_specs=[smem] + [vmem] * 13 + [smem],
        out_specs=vmem,
        scratch_shapes=[
            pltpu.VMEM((n_i + n_j, 64, res), BF16),
            pltpu.VMEM((n_i, 128, res), BF16),
            pltpu.VMEM((n_i, 128, res), BF16),
        ],
        compiler_params=pltpu.CompilerParams(vmem_limit_bytes=48 * 2**20),
        name="pair_block",
    )(
        starts, left3, rrhs, wp3, base, wd1, rel, tri_gain[:, None],
        sides[0], sides[1], w_gate, jnp.concatenate([w_tri_out, w_tri_out], axis=0),
        out_gain[:, None, None], mask.astype(F32)[None], mask,
    )
    rows = n_i // 2
    theirs = lax.dynamic_slice_in_dim(block, (1 - core) * rows, rows, 0)
    own = lax.dynamic_slice_in_dim(block, core * rows, rows, 0)
    other = partner(theirs, "core", NC, 1)
    return jnp.where(
        core == 0, jnp.concatenate([own, other], axis=1), jnp.concatenate([other, own], axis=1)
    )


def pair_vectors(states, token_start, lnf_gain, w_pair, pair_start):
    count = states.shape[0]
    mp = lax.axis_index("mp")
    weight = lnf_gain[:, None] * w_pair.astype(F32)
    high, low = split(weight)
    table = jnp.concatenate([high, low, jnp.ones((weight.shape[0], 8), BF16)], axis=1)
    dots = lax.dot_general(table, states, (((0,), (1,)), ((), ())), preferred_element_type=F32)
    states32 = states.astype(F32)
    second = jnp.sum(states32 * states32, axis=1)
    lanes = count // NY
    shift_row = jnp.pad(jnp.sum(weight, axis=0), (0, lanes - 64))
    rows = jnp.concatenate([dots[:64] + dots[64:128], dots[128:129], second[None]], axis=0)
    parts = jnp.concatenate(
        [
            jnp.swapaxes(rows.reshape(66, NY, lanes), 0, 1),
            jnp.broadcast_to(shift_row, (NY, 1, lanes)),
            jnp.zeros((NY, 5, lanes), F32),
        ],
        axis=1,
    )
    total = lax.dynamic_index_in_dim(parts, mp, 0, False)
    for by in range(1, NY):
        total = total + shift(
            lax.dynamic_index_in_dim(parts, (mp + by) % NY, 0, False), "mp", NY, by
        )
    full_width = weight.shape[0] * NY
    center = total[64] / full_width
    spread = total[65] / full_width - center * center
    vectors = (total[:64] - total[66, :64][:, None] * center[None]) * lax.rsqrt(spread + EPS)[None]
    place = token_start + mp * lanes + jnp.arange(lanes, dtype=jnp.int32)
    wanted = (place >= pair_start) & (place < pair_start + count)
    vectors = jnp.where(wanted[None], vectors, 0.0)
    vectors = vectors + partner(vectors, "core", NC, 1)
    for bit in (1, 2):
        vectors = vectors + partner(vectors, "x", NX, bit)
    for bit in (1, 2, 4):
        vectors = vectors + partner(vectors, "z", NZ, bit)
    around = [vectors] + [shift(vectors, "mp", NY, -by) for by in range(1, NY)]
    ring = jnp.concatenate(around + around, axis=1)
    return lax.dynamic_slice_in_dim(ring, (pair_start - mp * lanes) % count, count, 1)


def shards(
    tokens,
    ln1_gain,
    w_query,
    w_key,
    w_value,
    w_out,
    segment_ids,
    lnf_gain,
    w_pair,
    pair_start,
    residue_mask,
    w_pair_out,
    rel_table,
    tri_gain,
    w_ap,
    w_ag,
    w_bp,
    w_bg,
    w_gate,
    out_gain,
    w_tri_out,
):
    mp_index = lax.axis_index("mp")
    seq_index = (lax.axis_index("z") * NX + lax.axis_index("x")) * NC + lax.axis_index("core")
    count = tokens.shape[0]
    normed_tokens = norm_rows(tokens.astype(F32), ln1_gain).astype(BF16)
    own = w_query.shape[1]
    weights = lax.all_gather(
        jnp.concatenate([w_query, w_key, w_value], axis=1), SEQ, axis=0, tiled=True
    )
    sides = lax.all_gather(jnp.stack([w_ag.T, w_ap.T, w_bg.T, w_bp.T]), "mp", axis=1, tiled=True)
    sides = (sides[:2].reshape(128, 128), sides[2:].reshape(128, 128))
    projected = jnp.dot(normed_tokens, weights, preferred_element_type=F32)
    mixed = attend(
        projected[:, :own], projected[:, own : 2 * own], projected[:, 2 * own :], segment_ids[0], HD
    )
    local_width = w_out.shape[1]
    total = lax.dynamic_slice_in_dim(tokens, mp_index * local_width, local_width, 1).astype(F32)
    for by in range(NY):
        block = shift(mixed, "mp", NY, by) if by else mixed
        rows = lax.dynamic_slice_in_dim(w_out, (mp_index - by) % NY * own, own, 0)
        total = total + jnp.dot(block, rows, preferred_element_type=F32)
    final_states = total.astype(BF16)
    pair_t = pair_vectors(final_states, seq_index * count, lnf_gain, w_pair, pair_start[0])
    pair_update = pair_phase(
        pair_t, w_pair_out, rel_table, tri_gain, sides, w_gate, w_tri_out, out_gain, residue_mask
    )
    return (final_states, pair_update)


def solution(mesh):
    split_mesh = Mesh(mesh.devices.reshape(NZ, NX, NC, NY), ("z", "x", "core", "mp"))
    return jax.shard_map(
        shards,
        mesh=split_mesh,
        in_specs=(
            P(SEQ, None),
            P(),
            P(SEQ, "mp"),
            P(SEQ, "mp"),
            P(SEQ, "mp"),
            P(None, "mp"),
            P(SEQ, None),
            P("mp"),
            P("mp", None),
            P(),
            P(),
            P(),
            P(),
            P(),
            P(None, "mp"),
            P(None, "mp"),
            P(None, "mp"),
            P(None, "mp"),
            P(),
            P(),
            P(),
        ),
        out_specs=(P(SEQ, "mp"), P(SEQ, "mp", None)),
        check_vma=False,
    )
```

time: 746 us -> 296 us (0.40)
  waiting for transfers between devices: 562 us -> 149 us
  blocking collectives: 75.6 us -> 11.9 us
  Pallas kernels: 0 us -> 43.9 us
  matrix products: 57.9 us -> 30.6 us
  starting transfers between devices: 1.12 us -> 20.6 us
    all_gather x5 -> x1, waiting for transfers between devices: 325 us -> 101 us  [shards(): lax.all_gather(jnp.concatenate([w_query, w_key, w_value], axis=1), SEQ, a...]
    psum x1 -> x0, waiting for transfers between devices: 167 us -> none  [shards(): lax.psum((partial_value, first, second, shift_row), ('seq', 'mp'))]
    psum x1 -> x0, blocking collectives: 75.6 us -> none  [shards(): lax.psum((partial_value, first, second, shift_row), ('seq', 'mp'))]
    unnamed x12 -> x1, waiting for transfers between devices: 70.9 us -> 0.02 us
    ppermute x0 -> x16, waiting for transfers between devices: none -> 48.1 us  [the longest x9 31.1 us: shift(): lax.ppermute(value, axis, [(i, (i + by) % size) for i in range(size)])]
    pallas_call x0 -> x1, Pallas kernels: none -> 43.9 us  [pair_phase(): pl.pallas_call(pair_kernel, out_shape=jax.ShapeDtypeStruct((n_i, n_j, 128...]
    dot_general x19 -> x8, matrix products: 57.9 us -> 30.6 us  [the longest x1 17.1 us: shards(): projected = jnp.dot(normed_tokens, weights, preferred_element_type=F32)]
    ppermute x0 -> x16, starting transfers between devices: none -> 20.5 us  [the longest x9 12.8 us: shift(): lax.ppermute(value, axis, [(i, (i + by) % size) for i in range(size)])]
  transfers between devices with their start and end apart: 9 -> 17, of which waited for: 9 -> 13; matrix products, arithmetic and copies ran while one was open for 5% -> 6% of each run, Pallas kernels for 0% -> 0%
where the time goes in v1:
time: 296 us; the launch traced here: 293 us
  waiting for transfers between devices  149 us (50%)
  Pallas kernels  43.9 us (15%)
  matrix products  30.6 us (10%)
  starting transfers between devices  20.6 us (7%)
  between operations  15.4 us (5%)
  other arithmetic  13.8 us (5%)
  blocking collectives  11.9 us (4%)
  local copies, waits for them, and re-layouts  8.11 us (3%)
    all_gather x1, waiting for transfers between devices, shards(): lax.all_gather(jnp.concatenate([w_query, w_key, w_value], axis=1), SEQ, a...  101 us
    pallas_call x1, Pallas kernels, pair_phase(): pl.pallas_call(pair_kernel, out_shape=jax.ShapeDtypeStruct((n_i, n_j, 128...  43.9 us
    ppermute x9, waiting for transfers between devices, shift(): lax.ppermute(value, axis, [(i, (i + by) % size) for i in range(size)])  31.1 us
    dot_general x1, matrix products, shards(): projected = jnp.dot(normed_tokens, weights, preferred_element_type=F32)  17.1 us
    ppermute x7, waiting for transfers between devices, partner(): return lax.ppermute(value, axis, [(i, i ^ bit) for i in range(size)])  16.9 us
    ppermute x9, starting transfers between devices, shift(): lax.ppermute(value, axis, [(i, (i + by) % size) for i in range(size)])  12.8 us
    all_gather x1, blocking collectives, shards(): lax.all_gather(jnp.stack([w_ag.T, w_ap.T, w_bg.T, w_bp.T]), 'mp', axis=1,...  11.9 us
    dot_general x4, matrix products, shards(): total = total + jnp.dot(block, rows, preferred_element_type=F32)  11.3 us
  transfers between devices with their start and end apart: 17, of which 13 were waited for; matrix products, arithmetic and copies ran while one was open for 6% of the time, Pallas kernels for 0%

profile of v1, /device:TPU:2, one launch (start us, length us, event | category | flops | bytes accessed | tf_op | source)
XLA Modules:
  0.0 293.5 jit_solution(2676884258271010050)
XLA Ops:
  7.2 1.7 pad_maximum_fusion
  11.4 3.4 %convert_reduce_fusion = f32[512]{0:T(512)S(1)} fusion(bf16[512,5120]{1,0:T(8,128)(2,1)} %param.21), kind=kLoop, calls=%fused_computation.2 | loop fusion | flops 5242368 | bytes 5244928 | tf_op jit(solution)/shard_map/reduce_sum | solution.py:31
  15.5 1.5 fusion.3
  18.9 101.2 %all-gather.2.cloned.1.call-done = bf16[5120,1920]{1,0:T(8,128)(2,1)} async-done(((bf16[80,1920]{1,0:T(8,128)(2,1)}), bf16[5120,1920]{1,0:T(8,128)(2,1)}) %all-gather.2.cloned.1.call-update) | async-done | bytes 19660816 | tf_op jit(solution)/shard_map/all_gather | solution.py:279
  120.1 17.1 %fusion.6 = f32[512,1920]{1,0:T(8,128)S(1)} fusion(bf16[5120,1920]{1,0:T(8,128)(2,1)} %all-gather.2.cloned.1.call-done, bf16[512,5120]{1,0:T(8,128)(2,1)} %param.21, f32[5120]{0:T(1024)S(1)} %copy-done.18, f32[512]{0:T(512)S(1)} %add_rsqrt_fusion, f32[512]{0:T(512)S(1)} %broadcast_multiply_fusion), kind=kOutput, calls=%fused_computation.8 | convolution fusion | flops 10079436800 | bytes 28860416 | tf_op jit(solution)/shard_map/dot_general | solution.py:284
  137.3 1.2 fusion.61
  138.5 1.1 copy.41
  140.0 1.7 copy.42
  143.2 2.5 fusion.64
  146.2 2.8 collective-permute-start.2
  150.9 1.1 collective-permute-start
  152.0 3.0 %convolution_add_fusion.1 = f32[512,1280]{1,0:T(8,128)S(1)} fusion(bf16[512,640]{0,1:T(8,128)(2,1)S(1)} %bitcast.94, bf16[2560,1280]{1,0:T(8,128)(2,1)} %param.26, s32[]{:T(128)S(6)} %select_n.91, bf16[512,5120]{1,0:T(8,128)(2,1)} %param.21, s32[]{:T(128)S(6)} %select_n.88), kind=kOutput, calls=%fused_computation.17 | convolution fusion | flops 840171520 | bytes 6225928 | tf_op jit(solution)/shard_map/dot_general | solution.py:293
  155.0 22.5 %collective-permute-done.2 = bf16[512,640]{0,1:T(8,128)(2,1)S(1)} collective-permute-done((bf16[512,640]{0,1:T(8,128)(2,1)S(1)}, bf16[512,640]{0,1:T(8,128)(2,1)S(1)}, u32[]{:S(2)}, u32[]{:S(2)}) %collective-permute-start.2) | collective-permute-done | bytes 655392 | tf_op jit(solution)/shard_map/ppermute | solution.py:18
  177.6 2.6 fusion.19
  180.2 2.6 fusion.21
  182.9 3.0 %multiply_reduce_fusion = (f32[512]{0:T(512)S(1)}, bf16[512,1280]{1,0:T(8,128)(2,1)S(1)}) fusion(f32[512,1280]{1,0:T(8,128)S(1)} %fusion.19, f32[512,1280]{1,0:T(8,128)S(1)} %fusion.21, f32[512,1280]{1,0:T(8,128)S(1)} %convolution_add_fusion.1, bf16[512,640]{0,1:T(8,128)(2,1)S(1)} %collective-permute-done, bf16[2560,1280]{1,0:T(8,128)(2,1)} %param.26, ...), kind=kOutput, calls=%fused_computation.21 | convolution fusion | flops 843447808 | bytes 11470852 | tf_op jit(solution)/shard_map/dot_general | solution.py:293
  186.8 3.7 %collective-permute-start.5 = (f32[72,128]{1,0:T(8,128)S(1)}, f32[72,128]{1,0:T(8,128)S(1)}, u32[]{:S(2)}, u32[]{:S(2)}) collective-permute-start(f32[72,128]{1,0:T(8,128)S(1)} %get-tuple-element.19), channel_id=1, source_target_pairs={{0,3},{1,0},{2,1},{3,2},{4,7},{5,4},{6,5},{7,6},{8,11},{9,8},{10,9... | collective-permute-start | bytes 110600 | tf_op jit(solution)/shard_map/ppermute | solution.py:18
  192.2 3.9 %collective-permute-done.4 = f32[72,128]{1,0:T(8,128)S(1)} collective-permute-done((f32[72,128]{1,0:T(8,128)S(1)}, f32[72,128]{1,0:T(8,128)S(1)}, u32[]{:S(2)}, u32[]{:S(2)}) %collective-permute-start.4) | collective-permute-done | bytes 36896 | tf_op jit(solution)/shard_map/ppermute | solution.py:18
  197.6 1.9 collective-permute-start.7
  199.5 2.1 collective-permute-done.7
  201.6 1.5 collective-permute-start.8
  203.1 11.9 %all_gather.7 = bf16[4,64,128]{2,1,0:T(8,128)(2,1)S(1)} all-gather(bf16[4,16,128]{2,1,0:T(8,128)(2,1)S(1)} %pad_maximum_fusion.5), channel_id=1, replica_groups=mesh['z'=8,'x'=4,'core'=2,'mp'=4] {'mp'}, dimensions={1}, use_global_device_ids=true | all-gather | bytes 81920 | tf_op jit(solution)/shard_map/all_gather | solution.py:282
  215.2 3.8 %collective-permute-done.9 = f32[64,128]{1,0:T(8,128)S(1)} collective-permute-done((f32[64,128]{1,0:T(8,128)S(1)}, f32[64,128]{1,0:T(8,128)S(1)}, u32[]{:S(2)}, u32[]{:S(2)}) %collective-permute-start.9) | collective-permute-done | bytes 32800 | tf_op jit(solution)/shard_map/ppermute | solution.py:22
  219.0 1.4 collective-permute-start.10
  220.5 3.6 %collective-permute-done.10 = f32[64,128]{1,0:T(8,128)S(1)} collective-permute-done((f32[64,128]{1,0:T(8,128)S(1)}, f32[64,128]{1,0:T(8,128)S(1)}, u32[]{:S(2)}, u32[]{:S(2)}) %collective-permute-start.10) | collective-permute-done | bytes 32800 | tf_op jit(solution)/shard_map/ppermute | solution.py:22
  224.1 2.7 collective-permute-start.11
  226.9 5.0 %collective-permute-done.11 = f32[64,128]{1,0:T(8,128)S(1)} collective-permute-done((f32[64,128]{1,0:T(8,128)S(1)}, f32[64,128]{1,0:T(8,128)S(1)}, u32[]{:S(2)}, u32[]{:S(2)}) %collective-permute-start.11) | collective-permute-done | bytes 32800 | tf_op jit(solution)/shard_map/ppermute | solution.py:22
  231.9 1.2 collective-permute-start.12
  234.7 1.1 collective-permute-start.14
  236.2 3.1 %collective-permute-done.13 = f32[64,128]{1,0:T(8,128)S(1)} collective-permute-done((f32[64,128]{1,0:T(8,128)S(1)}, f32[64,128]{1,0:T(8,128)S(1)}, u32[]{:S(2)}, u32[]{:S(2)}) %collective-permute-start.13) | collective-permute-done | bytes 32800 | tf_op jit(solution)/shard_map/ppermute | solution.py:18
  240.5 43.9 %pair_block.1 = bf16[16,64,128]{2,1,0:T(8,128)(2,1)S(1)} custom-call(s32[4]{0:T(128)S(1)} %pad_add_fusion.starts, f32[512,128]{1,0:T(8,128)S(1)} %copy.54.left_ref, bf16[128,512]{1,0:T(8,128)(2,1)S(1)} %concatenate.77.rrhs_ref, f32[128,128]{1,0:T(8,128)S(1)} %maximum_maximum_fusion.2.wp_ref, f32[128,128]{1,0:T(8,128)S(1)} %concatenate.79.base_ref, ...), custom_call_target="tpu_custom_call" | custom-call | tf_op jit(solution)/shard_map/pair_block/pallas_call | solution.py:183
  284.5 1.3 collective-permute-done.15
  (131 shorter events, 16.6 us)
Async XLA Ops:
  7.2 112.9 %all-gather.2.cloned.1.call-start = ((), (), s32[]{:S(2)}) async-start(), calls=%async_computation | async-start | bytes 19968000 | tf_op jit(solution)/shard_map/all_gather | solution.py:279
  11.4 4.0 %copy-start.2 = (bf16[512,5120]{1,0:T(8,128)(2,1)S(1)}, bf16[512,5120]{1,0:T(8,128)(2,1)}, u32[]{:S(2)}) copy-start(bf16[512,5120]{1,0:T(8,128)(2,1)} %param.21) | copy-start | bytes 15728644
  15.5 104.6 %copy-start.18 = (f32[5120]{0:T(1024)S(1)}, f32[5120]{0:T(1024)}, u32[]{:S(2)}) copy-start(f32[5120]{0:T(1024)} %param.22) | copy-start | bytes 61444
  145.7 3.4 %copy-start.10 = (bf16[64,128]{1,0:T(8,128)(2,1)S(1)}, bf16[64,128]{1,0:T(8,128)(2,1)}, u32[]{:S(2)}) copy-start(bf16[64,128]{1,0:T(8,128)(2,1)} %param.32) | copy-start | bytes 49156
  146.2 31.3 %collective-permute-start.2 = (bf16[512,640]{0,1:T(8,128)(2,1)S(1)}, bf16[512,640]{0,1:T(8,128)(2,1)S(1)}, u32[]{:S(2)}, u32[]{:S(2)}) collective-permute-start(bf16[512,640]{0,1:T(8,128)(2,1)S(1)} %bitcast.91), channel_id=1, source_target_pairs={{0,3},{1,0},{2,1},{3,2},{4,7},{5,4},{6,5},{7,6},{8,11},{9,8},{10,9... | collective-permute-start | bytes 1966088 | tf_op jit(solution)/shard_map/ppermute | solution.py:18
  149.2 31.0 %collective-permute-start.1 = (bf16[512,640]{0,1:T(8,128)(2,1)S(1)}, bf16[512,640]{0,1:T(8,128)(2,1)S(1)}, u32[]{:S(2)}, u32[]{:S(2)}) collective-permute-start(bf16[512,640]{0,1:T(8,128)(2,1)S(1)} %bitcast.92), channel_id=1, source_target_pairs={{0,2},{1,3},{2,0},{3,1},{4,6},{5,7},{6,4},{7,5},{8,10},{9,11},{10,... | collective-permute-start | bytes 1966088 | tf_op jit(solution)/shard_map/ppermute | solution.py:18
  150.9 32.0 %collective-permute-start = (bf16[512,640]{0,1:T(8,128)(2,1)S(1)}, bf16[512,640]{0,1:T(8,128)(2,1)S(1)}, u32[]{:S(2)}, u32[]{:S(2)}) collective-permute-start(bf16[512,640]{0,1:T(8,128)(2,1)S(1)} %bitcast.93), channel_id=1, source_target_pairs={{0,1},{1,2},{2,3},{3,0},{4,5},{5,6},{6,7},{7,4},{8,9},{9,10},{10,1... | collective-permute-start | bytes 1966088 | tf_op jit(solution)/shard_map/ppermute | solution.py:18
  182.9 3.1 %copy-start.6 = (bf16[1280,64]{0,1:T(8,128)(2,1)S(1)}, bf16[1280,64]{0,1:T(8,128)(2,1)}, u32[]{:S(2)}) copy-start(bf16[1280,64]{0,1:T(8,128)(2,1)} %get-tuple-element.15) | copy-start | bytes 491524
  182.9 3.1 %copy-start.7 = (bf16[1280,64]{0,1:T(8,128)(2,1)S(1)}, bf16[1280,64]{0,1:T(8,128)(2,1)}, u32[]{:S(2)}) copy-start(bf16[1280,64]{0,1:T(8,128)(2,1)} %get-tuple-element.16) | copy-start | bytes 491524
  185.9 47.6 %copy-start.3 = (bf16[512,1280]{1,0:T(8,128)(2,1)}, bf16[512,1280]{1,0:T(8,128)(2,1)S(1)}, u32[]{:S(2)}) copy-start(bf16[512,1280]{1,0:T(8,128)(2,1)S(1)} %get-tuple-element.36) | copy-start | bytes 3932164
  185.9 17.2 %copy-start.12 = (bf16[128,16]{0,1:T(8,128)(2,1)S(1)}, bf16[128,16]{0,1:T(8,128)(2,1)}, u32[]{:S(2)}) copy-start(bf16[128,16]{0,1:T(8,128)(2,1)} %param.37) | copy-start | bytes 12292
  185.9 17.2 %copy-start.13 = (bf16[128,16]{0,1:T(8,128)(2,1)S(1)}, bf16[128,16]{0,1:T(8,128)(2,1)}, u32[]{:S(2)}) copy-start(bf16[128,16]{0,1:T(8,128)(2,1)} %param.38) | copy-start | bytes 12292
  185.9 17.2 %copy-start.14 = (bf16[128,16]{0,1:T(8,128)(2,1)S(1)}, bf16[128,16]{0,1:T(8,128)(2,1)}, u32[]{:S(2)}) copy-start(bf16[128,16]{0,1:T(8,128)(2,1)} %param.35) | copy-start | bytes 12292
  185.9 17.1 %copy-start.15 = (bf16[128,16]{0,1:T(8,128)(2,1)S(1)}, bf16[128,16]{0,1:T(8,128)(2,1)}, u32[]{:S(2)}) copy-start(bf16[128,16]{0,1:T(8,128)(2,1)} %param.36) | copy-start | bytes 12292
  185.9 40.9 %copy-start.9 = (bf16[64,128]{1,0:T(8,128)(2,1)S(1)}, bf16[64,128]{1,0:T(8,128)(2,1)}, u32[]{:S(2)}) copy-start(bf16[64,128]{1,0:T(8,128)(2,1)} %param.41) | copy-start | bytes 49156
  186.0 47.4 %copy-start.16 = (f32[128]{0:T(128)S(1)}, f32[128]{0:T(128)}, u32[]{:S(2)}) copy-start(f32[128]{0:T(128)} %param.34) | copy-start | bytes 1540
  186.0 47.5 %copy-start.17 = (f32[64]{0:T(128)S(1)}, f32[64]{0:T(128)}, u32[]{:S(2)}) copy-start(f32[64]{0:T(128)} %param.40) | copy-start | bytes 772
  186.0 47.6 %copy-start.1 = (s32[512]{0:T(512)S(1)}, s32[512]{0:T(512)}, u32[]{:S(2)}) copy-start(s32[512]{0:T(512)} %mask_smem.1) | copy-start | bytes 6148
  186.6 53.8 %copy-start = (bf16[128,128]{1,0:T(8,128)(2,1)S(1)}, bf16[128,128]{1,0:T(8,128)(2,1)}, u32[]{:S(2)}) copy-start(bf16[128,128]{1,0:T(8,128)(2,1)} %wgate_ref.1) | copy-start | bytes 98308
  186.8 5.4 %collective-permute-start.5 = (f32[72,128]{1,0:T(8,128)S(1)}, f32[72,128]{1,0:T(8,128)S(1)}, u32[]{:S(2)}, u32[]{:S(2)}) collective-permute-start(f32[72,128]{1,0:T(8,128)S(1)} %get-tuple-element.19), channel_id=1, source_target_pairs={{0,3},{1,0},{2,1},{3,2},{4,7},{5,4},{6,5},{7,6},{8,11},{9,8},{10,9... | collective-permute-start | bytes 110600 | tf_op jit(solution)/shard_map/ppermute | solution.py:18
  190.5 5.6 %collective-permute-start.4 = (f32[72,128]{1,0:T(8,128)S(1)}, f32[72,128]{1,0:T(8,128)S(1)}, u32[]{:S(2)}, u32[]{:S(2)}) collective-permute-start(f32[72,128]{1,0:T(8,128)S(1)} %get-tuple-element.20), channel_id=1, source_target_pairs={{0,2},{1,3},{2,0},{3,1},{4,6},{5,7},{6,4},{7,5},{8,10},{9,11},{10,... | collective-permute-start | bytes 110600 | tf_op jit(solution)/shard_map/ppermute | solution.py:18
  190.5 5.6 %collective-permute-start.3 = (f32[72,128]{1,0:T(8,128)S(1)}, f32[72,128]{1,0:T(8,128)S(1)}, u32[]{:S(2)}, u32[]{:S(2)}) collective-permute-start(f32[72,128]{1,0:T(8,128)S(1)} %get-tuple-element.18), channel_id=1, source_target_pairs={{0,1},{1,2},{2,3},{3,0},{4,5},{5,6},{6,7},{7,4},{8,9},{9,10},{10,1... | collective-permute-start | bytes 110600 | tf_op jit(solution)/shard_map/ppermute | solution.py:18
  196.2 1.3 collective-permute-start.6
  197.6 4.0 %collective-permute-start.7 = (f32[64,128]{1,0:T(8,128)S(1)}, f32[64,128]{1,0:T(8,128)S(1)}, u32[]{:S(2)}, u32[]{:S(2)}) collective-permute-start(f32[64,128]{1,0:T(8,128)S(1)} %fusion.72), channel_id=1, source_target_pairs={{0,8},{8,0},{16,24},{24,16},{1,9},{9,1},{17,25},{25,17},{2,10},{10... | collective-permute-start | bytes 98312 | tf_op jit(solution)/shard_map/ppermute | solution.py:22
  201.6 13.4 %collective-permute-start.8 = (f32[64,128]{1,0:T(8,128)S(1)}, f32[64,128]{1,0:T(8,128)S(1)}, u32[]{:S(2)}, u32[]{:S(2)}) collective-permute-start(f32[64,128]{1,0:T(8,128)S(1)} %add.211), channel_id=1, source_target_pairs={{0,16},{8,24},{16,0},{24,8},{1,17},{9,25},{17,1},{25,9},{2,18},{10... | collective-permute-start | bytes 98312 | tf_op jit(solution)/shard_map/ppermute | solution.py:22
  215.0 4.0 %collective-permute-start.9 = (f32[64,128]{1,0:T(8,128)S(1)}, f32[64,128]{1,0:T(8,128)S(1)}, u32[]{:S(2)}, u32[]{:S(2)}) collective-permute-start(f32[64,128]{1,0:T(8,128)S(1)} %add.212), channel_id=1, source_target_pairs={{0,32},{32,0},{64,96},{96,64},{128,160},{160,128},{192,224},{224,1... | collective-permute-start | bytes 98312 | tf_op jit(solution)/shard_map/ppermute | solution.py:22
  219.0 5.1 %collective-permute-start.10 = (f32[64,128]{1,0:T(8,128)S(1)}, f32[64,128]{1,0:T(8,128)S(1)}, u32[]{:S(2)}, u32[]{:S(2)}) collective-permute-start(f32[64,128]{1,0:T(8,128)S(1)} %add.213), channel_id=1, source_target_pairs={{0,64},{32,96},{64,0},{96,32},{128,192},{160,224},{192,128},{224,1... | collective-permute-start | bytes 98312 | tf_op jit(solution)/shard_map/ppermute | solution.py:22
  224.1 7.8 %collective-permute-start.11 = (f32[64,128]{1,0:T(8,128)S(1)}, f32[64,128]{1,0:T(8,128)S(1)}, u32[]{:S(2)}, u32[]{:S(2)}) collective-permute-start(f32[64,128]{1,0:T(8,128)S(1)} %add.214), channel_id=1, source_target_pairs={{0,128},{32,160},{64,192},{96,224},{128,0},{160,32},{192,64},{224,... | collective-permute-start | bytes 98312 | tf_op jit(solution)/shard_map/ppermute | solution.py:22
  231.9 4.2 %collective-permute-start.12 = (f32[64,128]{1,0:T(8,128)S(1)}, f32[64,128]{1,0:T(8,128)S(1)}, u32[]{:S(2)}, u32[]{:S(2)}) collective-permute-start(f32[64,128]{1,0:T(8,128)S(1)} %get-tuple-element.3), channel_id=1, source_target_pairs={{0,3},{1,0},{2,1},{3,2},{4,7},{5,4},{6,5},{7,6},{8,11},{9,8},{10,9... | collective-permute-start | bytes 98312 | tf_op jit(solution)/shard_map/ppermute | solution.py:18
  233.8 5.5 %collective-permute-start.13 = (f32[64,128]{1,0:T(8,128)S(1)}, f32[64,128]{1,0:T(8,128)S(1)}, u32[]{:S(2)}, u32[]{:S(2)}) collective-permute-start(f32[64,128]{1,0:T(8,128)S(1)} %get-tuple-element.3), channel_id=1, source_target_pairs={{0,2},{1,3},{2,0},{3,1},{4,6},{5,7},{6,4},{7,5},{8,10},{9,11},{10,... | collective-permute-start | bytes 98312 | tf_op jit(solution)/shard_map/ppermute | solution.py:18
  234.7 5.1 %collective-permute-start.14 = (f32[64,128]{1,0:T(8,128)S(1)}, f32[64,128]{1,0:T(8,128)S(1)}, u32[]{:S(2)}, u32[]{:S(2)}) collective-permute-start(f32[64,128]{1,0:T(8,128)S(1)} %get-tuple-element.3), channel_id=1, source_target_pairs={{0,1},{1,2},{2,3},{3,0},{4,5},{5,6},{6,7},{7,4},{8,9},{9,10},{10,1... | collective-permute-start | bytes 98312 | tf_op jit(solution)/shard_map/ppermute | solution.py:18
  284.4 1.4 collective-permute-start.15
  (4 other events, 10.0 us)
Sparse Core Ops, SparseCore 0:
  11.3 108.7 all-gather.1
